TPU v7x, 32 devices: a whole 2x2x4 slice. The times are simulated.
32 devices in a mesh: group: 2 (over y), row: 4 (over z), head: 2 (over x), sub: 2 (over core).
Axes of the slice: x: 2, y: 2, z: 4, core: 2. Of those that a mesh axis runs over, the one named last changes fastest.
Arguments:
- prior_state: float32 [64, 32, 128, 128], P(('group', 'row'), 'head', None, 'sub'), parts along dimension 0, may hold values from -6 to 6
- queries: bfloat16 [2, 64, 32, 128], P(None, ('group', 'row'), 'head'), parts along dimension 1, may hold values from -6 to 6
- new_keys: bfloat16 [2, 64, 32, 128], P(None, ('group', 'row'), 'head'), parts along dimension 1, may hold values from -6 to 6
- new_values: bfloat16 [2, 64, 32, 128], P(None, ('group', 'row'), 'head', 'sub'), parts along dimension 1, may hold values from -6 to 6
- out_gates: bfloat16 [2, 64, 32, 128], P(None, ('group', 'row'), 'head', 'sub'), parts along dimension 1, may hold values from -6 to 6
- decay_rates: float32 [32], P('head'), may hold values from 0.3 to 0.98
- norm_gain: float32 [32, 128], P('head', 'sub'), may hold values from 0.1 to 1.9
- out_weight: bfloat16 [32, 128, 3072], P('head', 'sub'), may hold values from -0.09375 to 0.09375
- residual: bfloat16 [2, 64, 3072], P(None, ('group', 'row')), parts along dimension 1, may hold values from -4 to 4
- ffn_gain: float32 [3072], replicated, may hold values from 0.1 to 1.9
- router_weight: bfloat16 [3072, 4], replicated, may hold values from -0.109375 to 0.109375
- gate_weight: bfloat16 [3072, 32768], P(None, ('row', 'head', 'sub')), may hold values from -0.109375 to 0.109375
- up_weight: bfloat16 [3072, 32768], P(None, ('row', 'head', 'sub')), may hold values from -0.109375 to 0.109375
- down_weight: bfloat16 [32768, 3072], P(('row', 'head', 'sub')), may hold values from -0.0625 to 0.0625
- expert_picks: int32 [2, 64, 2], P(None, ('group', 'row')), parts along dimension 1, may hold values from 0 to 3, all different within a row; in each aligned block of 8 rows (0 to 7, 8 to 15, ..., all dimensions but the last counted through in order) at most 6 rows name the same one
- finished: int32 [2, 64], P(None, ('group', 'row')), parts along dimension 1, may hold values from 0 to 1, as said below
- dest_slots: int32 [2, 64], P(None, ('group', 'row')), parts along dimension 1, may hold values from 0 to 31, as said below
Outputs:
- layer_out: bfloat16 [2, 64, 3072], P(None, ('group', 'row'), ('head', 'sub')), parts along dimension 1
There are 2 independent parts, one for each index of `group`. A program takes and returns all parts, laid end to end along the dimension named above; an argument that names none is the same for every part. Nothing has to cross between parts.
Inputs may be any that keep to these rules, and one draw needn't show every extreme that they name: `expert_picks`: in each step, the rows of one index of row name one expert at most 6 times, and the two picks of a row differ. A row finished at the first step is finished at the second. `dest_slots`: for each step a permutation of the rows of the group; rows that are not finished take the lowest slots.
All inputs are finite; a program needn't handle non-finite values.
Results may differ from a plain program's by a relative error of at most 0.0063.
Values may be sent and summed in bfloat16 or wider, within the bound.
A program may use at most 128 MiB of HBM per device.

v0:
```python
import jax
import jax.numpy as jnp
from jax import lax
from jax.sharding import PartitionSpec as P

HEADS = 32
HEAD_DIM = 128
STEPS = 2
CAP = 6


EPSILON = 1e-06


def expert_pass(received, gate_weight, up_weight, down_weight):
    gate_pre = jnp.einsum("scd,df->scf", received, gate_weight, preferred_element_type=jnp.float32)
    upward = jnp.einsum("scd,df->scf", received, up_weight, preferred_element_type=jnp.float32)
    hidden = (jax.nn.silu(gate_pre) * upward).astype(jnp.bfloat16)
    return jnp.einsum("scf,fd->scd", hidden, down_weight, preferred_element_type=jnp.float32)


def local(
    prior_state,
    queries,
    new_keys,
    new_values,
    out_gates,
    decay_rates,
    norm_gain,
    out_weight,
    residual,
    ffn_gain,
    router_weight,
    gate_weight,
    up_weight,
    down_weight,
    expert_picks,
    finished,
    dest_slots,
):
    row_devices = lax.axis_size("row")
    rows_here = queries.shape[1]
    experts = router_weight.shape[1]
    owners = row_devices // experts
    model_width = residual.shape[2]
    share_width = model_width // lax.axis_size(("head", "sub"))
    offset = lax.axis_index(("head", "sub")) * share_width
    expert_ids = lax.iota(jnp.int32, experts)
    slot_ids = lax.iota(jnp.int32, CAP)
    target_ids = lax.iota(jnp.int32, row_devices * rows_here)
    current = prior_state
    outputs = []
    for step_index in range(STEPS):
        keys_now = new_keys[step_index].astype(jnp.float32)
        values_now = new_values[step_index].astype(jnp.float32)
        query_now = queries[step_index].astype(jnp.float32)
        current = (
            decay_rates[None, :, None, None] * current
            + keys_now[:, :, :, None] * values_now[:, :, None, :]
        )
        attended = jnp.einsum("rhk,rhkv->rhv", query_now, current, precision=lax.Precision.HIGHEST)
        squares = jnp.sum(attended * attended, axis=(1, 2))
        gated_out = (
            attended * norm_gain[None] * jax.nn.sigmoid(out_gates[step_index].astype(jnp.float32))
        ).astype(jnp.bfloat16)
        partial_proj = jnp.einsum(
            "rhv,hvd->rd", gated_out, out_weight, preferred_element_type=jnp.float32
        )
        proj_sum, square_sum = lax.psum((partial_proj, squares), ("head", "sub"))
        mixed_rows = (
            residual[step_index].astype(jnp.float32)
            + proj_sum * lax.rsqrt(square_sum / (HEADS * HEAD_DIM) + EPSILON)[:, None]
        )
        normed = (
            mixed_rows
            * lax.rsqrt(jnp.mean(mixed_rows * mixed_rows, axis=1, keepdims=True) + EPSILON)
            * ffn_gain
        ).astype(jnp.bfloat16)
        logits = jnp.dot(normed, router_weight, preferred_element_type=jnp.float32)
        picks_now = expert_picks[step_index]
        chosen = picks_now[:, :, None] == expert_ids[None, None, :]
        picked_logits = jnp.sum(jnp.where(chosen, logits[:, None, :], 0.0), axis=2)
        first_weight = jax.nn.sigmoid(picked_logits[:, 0] - picked_logits[:, 1])
        second_weight = jax.nn.sigmoid(picked_logits[:, 1] - picked_logits[:, 0])
        mix_weights = jnp.stack([first_weight, second_weight], axis=1)
        live_flags = 1 - finished[step_index]
        alive_rows = live_flags.astype(jnp.float32)
        route_flags = chosen.astype(jnp.int32) * live_flags[:, None, None]
        flat_flags = route_flags.reshape(rows_here * 2, experts)
        position = jnp.cumsum(flat_flags, axis=0) - flat_flags
        placed = flat_flags[:, :, None] * (position[:, :, None] == slot_ids[None, None, :]).astype(
            jnp.int32
        )
        placed = placed.reshape(rows_here, 2, experts, CAP)
        selection = jnp.sum(placed, axis=1)
        weighted = jnp.sum(placed.astype(jnp.float32) * mix_weights[:, :, None, None], axis=1)
        buckets = jnp.einsum(
            "rec,rd->ecd",
            selection.astype(jnp.bfloat16),
            normed,
            preferred_element_type=jnp.float32,
        ).astype(jnp.bfloat16)
        outgoing = jnp.repeat(buckets, owners, axis=0, total_repeat_length=row_devices)
        produced = expert_pass(
            lax.all_to_all(outgoing, "row", split_axis=0, concat_axis=0, tiled=True),
            gate_weight,
            up_weight,
            down_weight,
        )
        back_rows = lax.all_to_all(produced, "row", split_axis=0, concat_axis=0, tiled=True)
        per_expert = back_rows.reshape(experts, owners, CAP, back_rows.shape[2]).sum(axis=1)
        combined = jnp.einsum("rec,ecd->rd", weighted, per_expert, precision=lax.Precision.HIGHEST)
        moe_share = lax.psum_scatter(combined, ("head", "sub"), scatter_dimension=1, tiled=True)
        mixed_share = lax.dynamic_slice_in_dim(mixed_rows, offset, share_width, 1)
        final_rows = ((mixed_share + moe_share) * alive_rows[:, None]).astype(jnp.bfloat16)
        mover_table = (dest_slots[step_index][None, :] == target_ids[:, None]).astype(jnp.bfloat16)
        leaving = jnp.dot(mover_table, final_rows, preferred_element_type=jnp.float32).astype(
            jnp.bfloat16
        )
        leaving = leaving.reshape(row_devices, rows_here, share_width)
        arrived = lax.all_to_all(leaving, "row", split_axis=0, concat_axis=0, tiled=True)
        outputs.append(jnp.sum(arrived.astype(jnp.float32), axis=0).astype(jnp.bfloat16))
    return jnp.stack(outputs, axis=0)


def solution(mesh):
    in_specs = (
        P(("group", "row"), "head", None, "sub"),
        P(None, ("group", "row"), "head", None),
        P(None, ("group", "row"), "head", None),
        P(None, ("group", "row"), "head", "sub"),
        P(None, ("group", "row"), "head", "sub"),
        P("head"),
        P("head", "sub"),
        P("head", "sub", None),
        P(None, ("group", "row"), None),
        P(),
        P(),
        P(None, ("row", "head", "sub")),
        P(None, ("row", "head", "sub")),
        P(("row", "head", "sub"), None),
        P(None, ("group", "row"), None),
        P(None, ("group", "row")),
        P(None, ("group", "row")),
    )
    out_specs = P(None, ("group", "row"), ("head", "sub"))
    return jax.shard_map(local, mesh=mesh, in_specs=in_specs, out_specs=out_specs, check_vma=False)
```

profile of v0, /device:TPU:0, one launch (start us, length us, event | category | flops | bytes accessed | tf_op | source)
XLA Modules:
  0.0 190.7 jit_solution(3291247213297383380)
XLA Ops:
  6.5 0.8 bitcast_convert_fusion.2
  7.3 0.8 bitcast_convert_fusion.3
  8.2 0.8 slice_bitcast_fusion.1
  9.0 5.6 %fusion.16 = f32[8,16,1,64]{3,2,1,0:T(1,128)S(1)} fusion(f32[8,16,128,64]{2,3,1,0:T(8,128)} %param.23, f32[8,16,64]{2,1,0:T(8,128)S(1)} %get-tuple-element.44, f32[8,16,128]{2,1,0:T(8,128)S(1)} %get-tuple-element.42, f32[16]{0:T(128)} %param.28, bf16[8,16,128,1]{2,1,0,3:T(8,128)(2,1)S(1)} %get-tuple-element.40), kind=kOutput, calls=%fused_computation.19 | convolution fusion | flops 15728640 | bytes 4358208 | tf_op jit(solution)/shard_map/rhk,rhkv->rhv/dot_general | solution.py:61
  14.5 6.5 %fusion.12 = f32[8,16,1,64]{3,2,1,0:T(1,128)S(1)} fusion(f32[8,16,128,64]{2,3,1,0:T(8,128)} %param.23, f32[8,16,64]{2,1,0:T(8,128)S(1)} %get-tuple-element.45, f32[8,16,128]{2,1,0:T(8,128)S(1)} %get-tuple-element.43, f32[8,16,64]{2,1,0:T(8,128)S(1)} %get-tuple-element.44, f32[8,16,128]{2,1,0:T(8,128)S(1)} %get-tuple-element.42, f32[16]{0:T(128)} %param.28, ...), kind=kOutput, calls=%fused_computation.14 | convolution fusion | flops 18874368 | bytes 4456512 | tf_op jit(solution)/shard_map/rhk,rhkv->rhv/dot_general | solution.py:61
  21.3 1.6 convolution_bitcast_fusion.1
  22.9 1.6 convolution_bitcast_fusion.3
  26.9 8.4 %all-reduce = (f32[8]{0:T(128)S(1)}, f32[8]{0:T(128)S(1)}) all-reduce(f32[8]{0:T(128)S(1)} %get-tuple-element.38, f32[8]{0:T(128)S(1)} %get-tuple-element.39), channel_id=1, replica_groups=mesh['group'=2,'row'=4,'head'=2,'sub'=2] {'head','sub'}, use_global_device_ids=true, to_apply=%region_12.14 | all-reduce | flops 16 | bytes 128 | tf_op jit(solution)/shard_map/psum | solution.py:69
  35.2 24.0 %all-reduce.4.cloned.1.call-done = (f32[8,3072]{1,0:T(8,128)}, f32[8,3072]{1,0:T(8,128)}) async-done(((f32[8,3072]{1,0:T(8,128)}, f32[8,3072]{1,0:T(8,128)}), (f32[8,3072]{1,0:T(8,128)}, f32[8,3072]{1,0:T(8,128)})) %all-reduce.4.cloned.1.call-update) | async-done | bytes 196624 | tf_op jit(solution)/shard_map/psum | solution.py:69
  59.2 1.2 multiply_reduce_fusion.1
  61.3 1.2 gather_fusion.1
  62.5 4.6 %all-to-all-start.3 = ((bf16[4,6,3072]{2,1,0:T(8,128)(2,1)}), bf16[4,6,3072]{2,1,0:T(8,128)(2,1)S(1)}, u32[]{:S(2)}, u32[]{:S(2)}) async-start(bf16[4,6,3072]{2,1,0:T(8,128)(2,1)} %gather_fusion.1), calls=%async_computation.4 | async-start | bytes 393216 | tf_op jit(solution)/shard_map/all_to_all | solution.py:105
  67.6 1.2 gather_fusion
  68.9 4.5 %all-to-all-done.3 = bf16[4,6,3072]{2,1,0:T(8,128)(2,1)S(1)} async-done(((bf16[4,6,3072]{2,1,0:T(8,128)(2,1)}), bf16[4,6,3072]{2,1,0:T(8,128)(2,1)S(1)}, u32[]{:S(2)}, u32[]{:S(2)}) %all-to-all-start.3) | async-done | bytes 147488 | tf_op jit(solution)/shard_map/all_to_all | solution.py:105
  73.4 3.5 %all-to-all-start = ((bf16[4,6,3072]{2,1,0:T(8,128)(2,1)}), bf16[4,6,3072]{2,1,0:T(8,128)(2,1)S(1)}, u32[]{:S(2)}, u32[]{:S(2)}) async-start(bf16[4,6,3072]{2,1,0:T(8,128)(2,1)} %gather_fusion), calls=%async_computation | async-start | bytes 393216 | tf_op jit(solution)/shard_map/all_to_all | solution.py:105
  76.9 6.6 %fusion.8 = f32[4,6,2048]{2,1,0:T(8,128)S(1)} fusion(bf16[4,6,3072]{2,1,0:T(8,128)(2,1)S(1)} %all-to-all-done.3, bf16[3072,2048]{1,0:T(8,128)(2,1)} %param.34), kind=kOutput, calls=%fused_computation.10 | convolution fusion | flops 301989888 | bytes 12926976 | tf_op jit(solution)/shard_map/scd,df->scf/dot_general | solution.py:16
  83.6 12.9 %fusion = f32[4,6,3072]{2,1,0:T(8,128)} fusion(bf16[2048,3072]{1,0:T(8,128)(2,1)} %param.36, bf16[4,6,3072]{2,1,0:T(8,128)(2,1)S(1)} %all-to-all-done.3, bf16[3072,2048]{1,0:T(8,128)(2,1)} %param.35, f32[4,6,2048]{2,1,0:T(8,128)S(1)} %fusion.8), kind=kOutput, calls=%fused_computation.2 | convolution fusion | flops 604274688 | bytes 25804800 | tf_op jit(solution)/shard_map/scf,fd->scd/dot_general | solution.py:19
  96.4 4.9 %all-to-all-start.4 = ((f32[4,6,3072]{2,1,0:T(8,128)}), f32[4,6,3072]{2,1,0:T(8,128)S(1)}, u32[]{:S(2)}, u32[]{:S(2)}) async-start(f32[4,6,3072]{2,1,0:T(8,128)} %fusion), calls=%async_computation.5 | async-start | bytes 786432 | tf_op jit(solution)/shard_map/all_to_all | solution.py:110
  101.3 6.6 %fusion.10 = f32[4,6,2048]{2,1,0:T(8,128)S(1)} fusion(bf16[4,6,3072]{2,1,0:T(8,128)(2,1)S(1)} %all-to-all-done, bf16[3072,2048]{1,0:T(8,128)(2,1)} %param.34), kind=kOutput, calls=%fused_computation.12 | convolution fusion | flops 301989888 | bytes 12926976 | tf_op jit(solution)/shard_map/scd,df->scf/dot_general | solution.py:16
  108.0 12.8 %fusion.2 = f32[4,6,3072]{2,1,0:T(8,128)} fusion(bf16[2048,3072]{1,0:T(8,128)(2,1)} %param.36, bf16[4,6,3072]{2,1,0:T(8,128)(2,1)S(1)} %all-to-all-done, bf16[3072,2048]{1,0:T(8,128)(2,1)} %param.35, f32[4,6,2048]{2,1,0:T(8,128)S(1)} %fusion.10), kind=kOutput, calls=%fused_computation.4 | convolution fusion | flops 604274688 | bytes 25804800 | tf_op jit(solution)/shard_map/scf,fd->scd/dot_general | solution.py:19
  120.8 5.1 %all-to-all-start.1 = ((f32[4,6,3072]{2,1,0:T(8,128)}), f32[4,6,3072]{2,1,0:T(8,128)S(1)}, u32[]{:S(2)}, u32[]{:S(2)}) async-start(f32[4,6,3072]{2,1,0:T(8,128)} %fusion.2), calls=%async_computation.1 | async-start | bytes 786432 | tf_op jit(solution)/shard_map/all_to_all | solution.py:110
  126.1 1.3 convolution_bitcast_fusion
  127.5 7.3 %all-to-all-done.1 = f32[4,6,3072]{2,1,0:T(8,128)S(1)} async-done(((f32[4,6,3072]{2,1,0:T(8,128)}), f32[4,6,3072]{2,1,0:T(8,128)S(1)}, u32[]{:S(2)}, u32[]{:S(2)}) %all-to-all-start.1) | async-done | bytes 294944 | tf_op jit(solution)/shard_map/all_to_all | solution.py:110
  134.8 1.3 convolution_bitcast_fusion.2
  136.1 13.4 %reduce-scatter.5.cloned.1.call-done = f32[8,768]{1,0:T(8,128)} async-done(((f32[8,3072]{1,0:T(8,128)}), f32[8,768]{1,0:T(8,128)}) %reduce-scatter.5.cloned.1.call-update) | async-done | bytes 24592 | tf_op jit(solution)/shard_map/reduce_scatter | solution.py:113
  149.6 1.5 fusion.42
  151.1 4.6 %all-to-all-start.5 = ((bf16[4,8,768]{2,1,0:T(8,128)(2,1)}), bf16[4,8,768]{2,1,0:T(8,128)(2,1)S(1)}, u32[]{:S(2)}, u32[]{:S(2)}) async-start(bf16[4,8,768]{2,1,0:T(8,128)(2,1)} %fusion.42), calls=%async_computation.7 | async-start | bytes 98304 | tf_op jit(solution)/shard_map/all_to_all | solution.py:121
  155.7 16.0 %reduce-scatter.3.cloned.1.call-done = f32[8,768]{1,0:T(8,128)} async-done(((f32[8,3072]{1,0:T(8,128)}), f32[8,768]{1,0:T(8,128)}) %reduce-scatter.3.cloned.1.call-update) | async-done | bytes 24592 | tf_op jit(solution)/shard_map/reduce_scatter | solution.py:113
  171.7 1.5 fusion.41
  173.2 4.6 %all-to-all-start.2 = ((bf16[4,8,768]{2,1,0:T(8,128)(2,1)}), bf16[4,8,768]{2,1,0:T(8,128)(2,1)S(1)}, u32[]{:S(2)}, u32[]{:S(2)}) async-start(bf16[4,8,768]{2,1,0:T(8,128)(2,1)} %fusion.41), calls=%async_computation.3 | async-start | bytes 98304 | tf_op jit(solution)/shard_map/all_to_all | solution.py:121
  177.9 5.7 %all-to-all-done.2 = bf16[4,8,768]{2,1,0:T(8,128)(2,1)S(1)} async-done(((bf16[4,8,768]{2,1,0:T(8,128)(2,1)}), bf16[4,8,768]{2,1,0:T(8,128)(2,1)S(1)}, u32[]{:S(2)}, u32[]{:S(2)}) %all-to-all-start.2) | async-done | bytes 49184 | tf_op jit(solution)/shard_map/all_to_all | solution.py:121
  183.6 0.6 pad_maximum_fusion
  (78 shorter events, 4.2 us)
Async XLA Ops:
  6.5 54.0 %copy-start = (bf16[3072,4]{0,1:T(4,128)(2,1)S(1)}, bf16[3072,4]{0,1:T(4,128)(2,1)}, u32[]{:S(2)}) copy-start(bf16[3072,4]{0,1:T(4,128)(2,1)} %param.33) | copy-start | bytes 73732
  6.5 52.7 %all-reduce.4.cloned.1.call-start = ((), (), s32[]{:S(2)}) async-start(), calls=%async_computation.10 | async-start | bytes 393216 | tf_op jit(solution)/shard_map/psum | solution.py:69
  8.1 12.9 %copy-start.2 = (bf16[2,8,16,64]{3,2,1,0:T(8,128)(2,1)S(1)}, bf16[2,8,16,64]{3,2,1,0:T(8,128)(2,1)}, u32[]{:S(2)}) copy-start(bf16[2,8,16,64]{3,2,1,0:T(8,128)(2,1)} %param.27) | copy-start | bytes 98308
  8.1 12.9 %copy-start.4 = (f32[16,64]{1,0:T(8,128)S(1)}, f32[16,64]{1,0:T(8,128)}, u32[]{:S(2)}) copy-start(f32[16,64]{1,0:T(8,128)} %param.29) | copy-start | bytes 12292
  9.0 12.3 %slice-start = ((s8[6291456]{0:T(1024)(128)(4,1)}), s8[2097152]{0:T(1024)(128)(4,1)S(1)}, s32[]{:S(2)}) async-start(s8[6291456]{0:T(1024)(128)(4,1)} %bitcast.115), calls=%async_computation.11 | async-start | bytes 4194304
  14.5 6.7 %slice-start.1 = ((s8[6291456]{0:T(1024)(128)(4,1)}), s8[4194304]{0:T(1024)(128)(4,1)S(1)}, s32[]{:S(2)}) async-start(s8[6291456]{0:T(1024)(128)(4,1)} %bitcast.115), calls=%async_computation.12 | async-start | bytes 8388608
  21.3 3.3 %copy-start.5 = (s32[2,8,2]{1,2,0:T(2,128)S(1)}, s32[2,8,2]{1,2,0:T(2,128)}, u32[]{:S(2)}) copy-start(s32[2,8,2]{1,2,0:T(2,128)} %param.37) | copy-start | bytes 388
  21.3 3.4 %copy-start.6 = (s32[2,8]{1,0:T(2,128)S(1)}, s32[2,8]{1,0:T(2,128)}, u32[]{:S(2)}) copy-start(s32[2,8]{1,0:T(2,128)} %param.38) | copy-start | bytes 196
  21.3 37.9 %copy-start.1 = (bf16[2,8,3072]{2,1,0:T(8,128)(2,1)S(1)}, bf16[2,8,3072]{2,1,0:T(8,128)(2,1)}, u32[]{:S(2)}) copy-start(bf16[2,8,3072]{2,1,0:T(8,128)(2,1)} %param.31) | copy-start | bytes 294916
  21.3 39.1 %copy-start.3 = (f32[3072]{0:T(1024)S(1)}, f32[3072]{0:T(1024)}, u32[]{:S(2)}) copy-start(f32[3072]{0:T(1024)} %param.32) | copy-start | bytes 36868
  62.5 10.9 %all-to-all-start.3 = ((bf16[4,6,3072]{2,1,0:T(8,128)(2,1)}), bf16[4,6,3072]{2,1,0:T(8,128)(2,1)S(1)}, u32[]{:S(2)}, u32[]{:S(2)}) async-start(bf16[4,6,3072]{2,1,0:T(8,128)(2,1)} %gather_fusion.1), calls=%async_computation.4 | async-start | bytes 393216 | tf_op jit(solution)/shard_map/all_to_all | solution.py:105
  73.4 23.0 %all-to-all-start = ((bf16[4,6,3072]{2,1,0:T(8,128)(2,1)}), bf16[4,6,3072]{2,1,0:T(8,128)(2,1)S(1)}, u32[]{:S(2)}, u32[]{:S(2)}) async-start(bf16[4,6,3072]{2,1,0:T(8,128)(2,1)} %gather_fusion), calls=%async_computation | async-start | bytes 393216 | tf_op jit(solution)/shard_map/all_to_all | solution.py:105
  96.4 24.4 %all-to-all-start.4 = ((f32[4,6,3072]{2,1,0:T(8,128)}), f32[4,6,3072]{2,1,0:T(8,128)S(1)}, u32[]{:S(2)}, u32[]{:S(2)}) async-start(f32[4,6,3072]{2,1,0:T(8,128)} %fusion), calls=%async_computation.5 | async-start | bytes 786432 | tf_op jit(solution)/shard_map/all_to_all | solution.py:110
  107.9 28.2 %copy-start.7 = (s32[2,8]{1,0:T(2,128)S(1)}, s32[2,8]{1,0:T(2,128)}, u32[]{:S(2)}) copy-start(s32[2,8]{1,0:T(2,128)} %param.39) | copy-start | bytes 196
  120.8 14.0 %all-to-all-start.1 = ((f32[4,6,3072]{2,1,0:T(8,128)}), f32[4,6,3072]{2,1,0:T(8,128)S(1)}, u32[]{:S(2)}, u32[]{:S(2)}) async-start(f32[4,6,3072]{2,1,0:T(8,128)} %fusion.2), calls=%async_computation.1 | async-start | bytes 786432 | tf_op jit(solution)/shard_map/all_to_all | solution.py:110
  125.9 23.7 %reduce-scatter.5.cloned.1.call-start = ((), (), s32[]{:S(2)}) async-start(), calls=%async_computation.9 | async-start | bytes 122880 | tf_op jit(solution)/shard_map/reduce_scatter | solution.py:113
  127.4 44.3 %reduce-scatter.3.cloned.1.call-start = ((), (), s32[]{:S(2)}) async-start(), calls=%async_computation.8 | async-start | bytes 122880 | tf_op jit(solution)/shard_map/reduce_scatter | solution.py:113
  151.1 22.1 %all-to-all-start.5 = ((bf16[4,8,768]{2,1,0:T(8,128)(2,1)}), bf16[4,8,768]{2,1,0:T(8,128)(2,1)S(1)}, u32[]{:S(2)}, u32[]{:S(2)}) async-start(bf16[4,8,768]{2,1,0:T(8,128)(2,1)} %fusion.42), calls=%async_computation.7 | async-start | bytes 98304 | tf_op jit(solution)/shard_map/all_to_all | solution.py:121
  173.2 10.3 %all-to-all-start.2 = ((bf16[4,8,768]{2,1,0:T(8,128)(2,1)}), bf16[4,8,768]{2,1,0:T(8,128)(2,1)S(1)}, u32[]{:S(2)}, u32[]{:S(2)}) async-start(bf16[4,8,768]{2,1,0:T(8,128)(2,1)} %fusion.41), calls=%async_computation.3 | async-start | bytes 98304 | tf_op jit(solution)/shard_map/all_to_all | solution.py:121
Sparse Core Ops, SparseCore 0:
  24.7 34.4 all-reduce.3
  129.3 20.2 reduce-scatter.4
  152.1 19.5 reduce-scatter.2
where the time goes:
time: 192 us; the launch traced here: 191 us
  waiting for transfers between devices  70.9 us (37%)
  matrix products  60.6 us (32%)
  starting transfers between devices  27.4 us (14%)
  between operations  13.4 us (7%)
  blocking collectives  8.36 us (4%)
  other arithmetic  5.43 us (3%)
  local copies, waits for them, and re-layouts  4.68 us (2%)
    reduce_scatter x2, waiting for transfers between devices, local(): lax.psum_scatter(combined, ('head', 'sub'), scatter_dimension=1, tiled=True)  29.4 us
    dot_general x2, matrix products, expert_pass(): jnp.einsum('scf,fd->scd', hidden, down_weight, preferred_element_type=jnp...  25.7 us
    psum x1, waiting for transfers between devices, local(): proj_sum, square_sum = lax.psum((partial_proj, squares), ('head', 'sub'))  24 us
    dot_general x2, matrix products, expert_pass(): jnp.einsum('scd,df->scf', received, gate_weight, preferred_element_type=j...  13.3 us
    dot_general x2, matrix products, local(): jnp.einsum('rhk,rhkv->rhv', query_now, current, precision=lax.Precision.H...  12.1 us
    all_to_all x2, starting transfers between devices, local(): lax.all_to_all(produced, 'row', split_axis=0, concat_axis=0, tiled=True)  9.97 us
    all_to_all x2, starting transfers between devices, local(): lax.all_to_all(leaving, 'row', split_axis=0, concat_axis=0, tiled=True)  9.23 us
    psum x1, blocking collectives, local(): proj_sum, square_sum = lax.psum((partial_proj, squares), ('head', 'sub'))  8.36 us
  transfers between devices with their start and end apart: 9, of which 6 were waited for; matrix products, arithmetic and copies ran while one was open for 26% of the time, Pallas kernels for 0%

commit v1 on v0

v1 whole, which is shorter than its diff:
```python
import jax
import jax.numpy as jnp
from jax import lax
from jax.sharding import PartitionSpec as P

HEADS = 32
HEAD_DIM = 128
STEPS = 2


EPSILON = 1e-06


def local(
    prior_state,
    queries,
    new_keys,
    new_values,
    out_gates,
    decay_rates,
    norm_gain,
    out_weight,
    residual,
    ffn_gain,
    router_weight,
    gate_weight,
    up_weight,
    down_weight,
    expert_picks,
    finished,
    dest_slots,
):
    f32, bf16 = jnp.float32, jnp.bfloat16
    row_devices = lax.axis_size("row")
    shares = lax.axis_size(("head", "sub"))
    rows = queries.shape[1]
    experts = router_weight.shape[1]
    width = residual.shape[2]
    share_width = width // shares
    owners = row_devices // experts
    row_index = lax.axis_index("row")
    share_index = lax.axis_index(("head", "sub"))
    read = jnp.einsum(
        "srhk,rhkv->srhv", queries, prior_state.astype(bf16), preferred_element_type=f32
    )
    q, k, v = queries.astype(f32), new_keys.astype(f32), new_values.astype(f32)
    d = decay_rates[None, :, None]
    score = lambda s, t: jnp.sum(q[s] * k[t], axis=2, keepdims=True)
    first = d * read[0] + score(0, 0) * v[0]
    second = d * (d * read[1] + score(1, 0) * v[0]) + score(1, 1) * v[1]
    attended = jnp.stack([first, second])
    squares = jnp.sum(attended * attended, axis=(2, 3))
    gated = (attended * norm_gain * jax.nn.sigmoid(out_gates.astype(f32))).astype(bf16)
    partial = jnp.dot(
        gated.reshape(STEPS * rows, -1),
        out_weight.reshape(-1, width),
        preferred_element_type=f32,
    )
    proj, square_sum = lax.psum((partial, squares.reshape(STEPS * rows)), ("head", "sub"))
    mixed = (
        residual.reshape(STEPS * rows, width).astype(f32)
        + proj * lax.rsqrt(square_sum / (HEADS * HEAD_DIM) + EPSILON)[:, None]
    )
    normed = (
        mixed * lax.rsqrt(jnp.mean(mixed * mixed, axis=1, keepdims=True) + EPSILON) * ffn_gain
    ).astype(bf16)
    facts = jnp.concatenate(
        [expert_picks, finished[:, :, None], dest_slots[:, :, None]], axis=2
    ).reshape(STEPS * rows, 4)
    facts = lax.all_gather(facts, "row", axis=0, tiled=True)
    everyone = lax.all_gather(normed, "row", axis=0, tiled=True)
    logits = jnp.dot(everyone, router_weight, preferred_element_type=f32)
    expert_ids = lax.iota(jnp.int32, experts)[None, :]
    chosen_a = facts[:, 0:1] == expert_ids
    chosen_b = facts[:, 1:2] == expert_ids
    gap = jnp.sum(jnp.where(chosen_a, logits, 0.0), 1) - jnp.sum(jnp.where(chosen_b, logits, 0.0), 1)
    mine = row_index // owners
    share_of = jnp.where(facts[:, 0] == mine, jax.nn.sigmoid(gap), 0.0) + jnp.where(
        facts[:, 1] == mine, jax.nn.sigmoid(-gap), 0.0
    )
    share_of = share_of * (1 - facts[:, 2]).astype(f32)
    gate_pre = jnp.dot(everyone, gate_weight, preferred_element_type=f32)
    upward = jnp.dot(everyone, up_weight, preferred_element_type=f32)
    hidden = (jax.nn.silu(gate_pre) * upward * share_of[:, None]).astype(bf16)
    spots = lax.iota(jnp.int32, row_devices * STEPS * rows)
    spot_step = (spots // rows) % STEPS
    spot_slot = spots // (STEPS * rows) * rows + spots % rows
    mover = (spot_step[:, None] == spot_step[None, :]) & (spot_slot[:, None] == facts[None, :, 3])
    hidden = jnp.dot(mover.astype(bf16), hidden, preferred_element_type=f32).astype(bf16)
    produced = jnp.dot(hidden, down_weight, preferred_element_type=f32)
    own_step = lax.iota(jnp.int32, STEPS * rows) // rows
    own_mover = (spot_step[:, None] == own_step[None, :]) & (
        spot_slot[:, None] == dest_slots.reshape(-1)[None, :]
    )
    mixed_share = lax.dynamic_slice_in_dim(mixed, share_index * share_width, share_width, 1)
    mixed_share = mixed_share * (1 - finished).astype(f32).reshape(-1, 1)
    placed = jnp.dot(own_mover.astype(f32), mixed_share, precision=lax.Precision.HIGHEST)
    reduced = lax.psum_scatter(produced, ("head", "sub"), scatter_dimension=1, tiled=True)
    final = lax.psum_scatter(reduced + placed, "row", scatter_dimension=0, tiled=True)
    return final.astype(bf16).reshape(STEPS, rows, share_width)


def solution(mesh):
    in_specs = (
        P(("group", "row"), "head", None, "sub"),
        P(None, ("group", "row"), "head", None),
        P(None, ("group", "row"), "head", None),
        P(None, ("group", "row"), "head", "sub"),
        P(None, ("group", "row"), "head", "sub"),
        P("head"),
        P("head", "sub"),
        P("head", "sub", None),
        P(None, ("group", "row"), None),
        P(),
        P(),
        P(None, ("row", "head", "sub")),
        P(None, ("row", "head", "sub")),
        P(("row", "head", "sub"), None),
        P(None, ("group", "row"), None),
        P(None, ("group", "row")),
        P(None, ("group", "row")),
    )
    out_specs = P(None, ("group", "row"), ("head", "sub"))
    return jax.shard_map(local, mesh=mesh, in_specs=in_specs, out_specs=out_specs, check_vma=False)
```

time: 192 us -> 145 us (0.76)
  matrix products: 60.6 us -> 31.6 us
  starting transfers between devices: 27.4 us -> 0.12 us
  blocking collectives: 8.36 us -> 34.8 us
  waiting for transfers between devices: 70.9 us -> 57 us
  local copies, waits for them, and re-layouts: 4.68 us -> 0.75 us
    dot_general x16 -> x7, matrix products: 60.6 us -> 31.6 us  [the longest x1 7.94 us: local(): produced = jnp.dot(hidden, down_weight, preferred_element_type=f32)]
    all_to_all x6 -> x0, starting transfers between devices: 27.3 us -> none  [the longest x2 9.97 us: local(): lax.all_to_all(produced, 'row', split_axis=0, concat_axis=0, tiled=True)]
    all_gather x0 -> x2, blocking collectives: none -> 26.5 us  [the longest x1 14.4 us: local(): everyone = lax.all_gather(normed, 'row', axis=0, tiled=True)]
    all_to_all x6 -> x0, waiting for transfers between devices: 17.5 us -> none  [the longest x2 7.31 us: local(): lax.all_to_all(produced, 'row', split_axis=0, concat_axis=0, tiled=True)]
    reduce_scatter x2, waiting for transfers between devices: 29.4 us -> 43.4 us  [the longest x1 23.6 us: local(): lax.psum_scatter(produced, ('head', 'sub'), scatter_dimension=1, tiled=True)]
    psum x1, waiting for transfers between devices: 24 us -> 13.6 us  [local(): lax.psum((partial, squares.reshape(STEPS * rows)), ('head', 'sub'))]
    gather x2 -> x0, local copies, waits for them, and re-layouts: 2.47 us -> none  [local(): jnp.repeat(buckets, owners, axis=0, total_repeat_length=row_devices)]
  transfers between devices with their start and end apart: 9 -> 3, of which waited for: 6 -> 3; matrix products, arithmetic and copies ran while one was open for 26% -> 0% of each run, Pallas kernels for 0% -> 0%
where the time goes in v1:
time: 145 us
  waiting for transfers between devices  57 us (39%)
  blocking collectives  34.8 us (24%)
  matrix products  31.6 us (22%)
  between operations  13.2 us (9%)
  other arithmetic  7.22 us (5%)
    reduce_scatter x1, waiting for transfers between devices, local(): lax.psum_scatter(produced, ('head', 'sub'), scatter_dimension=1, tiled=True)  23.6 us
    reduce_scatter x1, waiting for transfers between devices, local(): lax.psum_scatter(reduced + placed, 'row', scatter_dimension=0, tiled=True)  19.8 us
    all_gather x1, blocking collectives, local(): everyone = lax.all_gather(normed, 'row', axis=0, tiled=True)  14.4 us
    psum x1, waiting for transfers between devices, local(): lax.psum((partial, squares.reshape(STEPS * rows)), ('head', 'sub'))  13.6 us
    all_gather x1, blocking collectives, local(): facts = lax.all_gather(facts, 'row', axis=0, tiled=True)  12.1 us
    psum x1, blocking collectives, local(): lax.psum((partial, squares.reshape(STEPS * rows)), ('head', 'sub'))  8.31 us
    dot_general x1, matrix products, local(): produced = jnp.dot(hidden, down_weight, preferred_element_type=f32)  7.94 us
    dot_general x1, matrix products, local(): upward = jnp.dot(everyone, up_weight, preferred_element_type=f32)  6.94 us
  transfers between devices with their start and end apart: 3, of which 3 were waited for; matrix products, arithmetic and copies ran while one was open for 0% of the time, Pallas kernels for 0%

profile of v1, /device:TPU:0, one launch (start us, length us, event | category | flops | bytes accessed | tf_op | source)
XLA Modules:
  0.0 144.8 jit_solution(14250250209717204223)
XLA Ops:
  6.6 0.9 convert_element_type.48
  7.5 0.9 convert_element_type.49
  8.4 3.4 %fusion.2 = f32[8,16,64,2]{2,3,1,0:T(2,128)S(1)} fusion(f32[8,16,128,64]{2,3,1,0:T(8,128)} %param.17, bf16[2,8,16,128]{3,2,1,0:T(8,128)(2,1)} %param.18), kind=kOutput, calls=%fused_computation.4 | convolution fusion | flops 5242880 | bytes 4325376 | tf_op jit(solution)/shard_map/srhk,rhkv->srhv/dot_general | solution.py:43
  11.8 0.9 convert_element_type.50
  12.6 0.1 fusion.9
  12.7 0.8 fusion.10
  13.5 1.0 multiply_reduce_fusion.1
  14.5 0.1 reshape.172
  14.6 4.4 %fusion.43 = f32[16,3072]{1,0:T(8,128)} fusion(bf16[16,1024]{1,0:T(8,128)(2,1)S(1)} %reshape.172, bf16[1024,3072]{1,0:T(8,128)(2,1)} %bitcast.44), kind=kOutput, calls=%fused_computation.81 | convolution fusion | flops 100663296 | bytes 6520832 | tf_op jit(solution)/shard_map/dot_general | solution.py:54
  19.1 0.0 reduce-scatter.3.cloned.1.call-start
  19.1 0.1 reshape.174
  19.2 8.3 %psum.15 = f32[16]{0:T(128)S(1)} all-reduce(f32[16]{0:T(128)S(1)} %reshape.174), channel_id=1, replica_groups=mesh['group'=2,'row'=4,'head'=2,'sub'=2] {'head','sub'}, use_global_device_ids=true, to_apply=%region_5.0 | all-reduce | flops 16 | bytes 128 | tf_op jit(solution)/shard_map/psum | solution.py:59
  27.5 0.1 concatenate.10
  27.6 0.1 concatenate.11
  27.7 0.1 concatenate.12
  27.8 12.1 %all-gather = s32[4,16,4]{1,2,0:T(4,128)S(1)} all-gather(s32[1,16,4]{1,2,0:T(4,128)S(1)} %add_bitcast_fusion), channel_id=1, replica_groups=mesh['group'=2,'row'=4,'head'=2,'sub'=2] {'row'}, dimensions={0}, use_global_device_ids=true | all-gather | bytes 1280 | tf_op jit(solution)/shard_map/all_gather | solution.py:70
  39.9 0.1 reshape.180
  40.0 13.6 %all-reduce.2.cloned.1.call-done = f32[16,3072]{1,0:T(8,128)} async-done(((f32[16,3072]{1,0:T(8,128)}), f32[16,3072]{1,0:T(8,128)}) %all-reduce.2.cloned.1.call-update) | async-done | bytes 196624 | tf_op jit(solution)/shard_map/psum | solution.py:59
  53.6 1.1 multiply_reduce_fusion
  54.8 0.1 multiply_convert_fusion
  54.8 14.4 %all_gather.7 = bf16[64,3072]{1,0:T(8,128)(2,1)S(1)} all-gather(bf16[16,3072]{1,0:T(8,128)(2,1)S(1)} %multiply_convert_fusion), channel_id=1, replica_groups=mesh['group'=2,'row'=4,'head'=2,'sub'=2] {'row'}, dimensions={0}, use_global_device_ids=true | all-gather | bytes 491520 | tf_op jit(solution)/shard_map/all_gather | solution.py:71
  69.2 6.9 %fusion.44 = f32[64,2048]{1,0:T(8,128)S(1)} fusion(bf16[64,3072]{1,0:T(8,128)(2,1)S(1)} %all_gather.7, bf16[3072,2048]{1,0:T(8,128)(2,1)} %param.28), kind=kOutput, calls=%fused_computation.82 | convolution fusion | flops 805306368 | bytes 13500416 | tf_op jit(solution)/shard_map/dot_general | solution.py:82
  76.1 0.2 select_reduce_fusion
  76.4 6.9 %fusion.1 = bf16[64,2048]{1,0:T(8,128)(2,1)S(1)} fusion(bf16[64,3072]{1,0:T(8,128)(2,1)S(1)} %all_gather.7, bf16[3072,2048]{1,0:T(8,128)(2,1)} %param.29, f32[64,2048]{1,0:T(8,128)S(1)} %fusion.44, f32[64]{0:T(128)S(1)} %fusion.41), kind=kOutput, calls=%fused_computation.2 | convolution fusion | flops 806223872 | bytes 13762816 | tf_op jit(solution)/shard_map/dot_general | solution.py:83
  83.3 7.9 %fusion.4 = f32[64,3072]{1,0:T(8,128)} fusion(bf16[2048,3072]{1,0:T(8,128)(2,1)} %param.30, bf16[64,2048]{1,0:T(8,128)(2,1)S(1)} %fusion.1, s32[64]{0:T(128)S(1)} %get-tuple-element.16, s32[64]{0:T(128)S(1)} %and_select_fusion.3, s32[64]{0:T(128)S(1)} %fusion.36), kind=kOutput, calls=%fused_computation.6 | convolution fusion | flops 822226944 | bytes 13632256 | tf_op jit(solution)/shard_map/dot_general | solution.py:90
  91.3 0.0 reduce-scatter.5.cloned.1.call-start
  91.4 0.1 eq.123
  91.4 0.1 mul.183
  91.5 23.6 %reduce-scatter.3.cloned.1.call-done = f32[64,768]{1,0:T(8,128)} async-done(((f32[64,3072]{1,0:T(8,128)}), f32[64,768]{1,0:T(8,128)}) %reduce-scatter.3.cloned.1.call-update) | async-done | bytes 196624 | tf_op jit(solution)/shard_map/reduce_scatter | solution.py:98
  115.1 1.9 %convolution_add_fusion = f32[64,768]{1,0:T(8,128)} fusion(f32[64,768]{1,0:T(8,128)} %reduce-scatter.3.cloned.1.call-done, f32[16,3072]{1,0:T(8,128)S(1)} %get-tuple-element.11, s32[]{:T(128)S(6)} %select_n.90, f32[16]{0:T(128)S(1)} %mul.183, s32[16]{0:T(128)S(1)} %eq.123, s32[16]{0:T(128)S(1)} %and_select_fusion, s32[64]{0:T(128)S(1)} %fusion.36, ...), kind=kOutput, calls=%fused_computation.7 | convolution fusion | flops 9501696 | bytes 444932 | tf_op jit(solution)/shard_map/dot_general | solution.py:97
  117.0 19.8 %reduce-scatter.5.cloned.1.call-done = f32[16,768]{1,0:T(8,128)} async-done(((f32[64,768]{1,0:T(8,128)}), f32[16,768]{1,0:T(8,128)}) %reduce-scatter.5.cloned.1.call-update) | async-done | bytes 49168 | tf_op jit(solution)/shard_map/reduce_scatter | solution.py:99
  136.8 1.4 convert_bitcast_fusion
  (28 shorter events, 0.2 us)
Async XLA Ops:
  6.5 69.6 %copy-start = (bf16[3072,4]{0,1:T(4,128)(2,1)S(1)}, bf16[3072,4]{0,1:T(4,128)(2,1)}, u32[]{:S(2)}) copy-start(bf16[3072,4]{0,1:T(4,128)(2,1)} %param.27) | copy-start | bytes 73732
  6.5 21.0 %copy-start.3 = (s32[2,8,2]{1,2,0:T(2,128)S(1)}, s32[2,8,2]{1,2,0:T(2,128)}, u32[]{:S(2)}) copy-start(s32[2,8,2]{1,2,0:T(2,128)} %param.31) | copy-start | bytes 388
  6.5 21.1 %copy-start.4 = (s32[2,8]{1,0:T(2,128)S(1)}, s32[2,8]{1,0:T(2,128)}, u32[]{:S(2)}) copy-start(s32[2,8]{1,0:T(2,128)} %param.32) | copy-start | bytes 196
  6.5 21.2 %copy-start.5 = (s32[2,8]{1,0:T(2,128)S(1)}, s32[2,8]{1,0:T(2,128)}, u32[]{:S(2)}) copy-start(s32[2,8]{1,0:T(2,128)} %param.33) | copy-start | bytes 196
  6.5 47.1 %copy-start.1 = (bf16[2,8,3072]{2,1,0:T(8,128)(2,1)S(1)}, bf16[2,8,3072]{2,1,0:T(8,128)(2,1)}, u32[]{:S(2)}) copy-start(bf16[2,8,3072]{2,1,0:T(8,128)(2,1)} %param.25) | copy-start | bytes 294916
  6.5 48.2 %copy-start.2 = (f32[3072]{0:T(1024)S(1)}, f32[3072]{0:T(1024)}, u32[]{:S(2)}) copy-start(f32[3072]{0:T(1024)} %param.26) | copy-start | bytes 36868
  6.6 47.0 %all-reduce.2.cloned.1.call-start = ((), (), s32[]{:S(2)}) async-start(), calls=%async_computation.2 | async-start | bytes 393216 | tf_op jit(solution)/shard_map/psum | solution.py:59
  19.1 96.1 %reduce-scatter.3.cloned.1.call-start = ((), (), s32[]{:S(2)}) async-start(), calls=%async_computation.3 | async-start | bytes 983040 | tf_op jit(solution)/shard_map/reduce_scatter | solution.py:98
  91.3 45.5 %reduce-scatter.5.cloned.1.call-start = ((), (), s32[]{:S(2)}) async-start(), calls=%async_computation.4 | async-start | bytes 245760 | tf_op jit(solution)/shard_map/reduce_scatter | solution.py:99
Sparse Core Ops, SparseCore 0:
  19.2 34.3 all-reduce.1
  91.4 23.6 reduce-scatter.2
  117.4 19.3 reduce-scatter.4

commit v2 on v1

--- a/solution.py
+++ b/solution.py
@@ -1,6 +1,10 @@
+import functools
+
 import jax
 import jax.numpy as jnp
 from jax import lax
+from jax.experimental import pallas as pl
+from jax.experimental.pallas import tpu as pltpu
 from jax.sharding import PartitionSpec as P
 
 HEADS = 32
@@ -100,6 +104,426 @@
     return final.astype(bf16).reshape(STEPS, rows, share_width)
 
 
+def high_low(value, lanes):
+    high = value.astype(jnp.bfloat16).astype(jnp.float32)
+    return jnp.where(lanes < 64, high, value - high)
+
+
+def column_of(ext):
+    return ext[:, 0:1].astype(jnp.float32) + ext[:, 64:65].astype(jnp.float32)
+
+
+def fused_kernel(
+    n,
+    experts,
+    decay_s,
+    q_h, k_h, v_h, g_h, gain_h, res_h, fgain_h, router_h, meta_h,
+    state_h, wo_h, wg_h, wu_h, wd_h,
+    out_ref,
+    q_b, k_b, v_b, g_b, gain_b, res_b, fgain_b, router_b,
+    state_b, wo_b, wg_b, wu_b, wd_b,
+    q32, k32, v32, g32, gated_b, facts_b, mix_b,
+    a_send, a_recv, x_all, acc_g, acc_u, hid_b, d_send, d_recv, y_b, y_send, y_recv,
+    small_sem, state_sem, wo_sem, wg_sem, wu_sem, wd_sem,
+    facts_ss, facts_rs, a_ss, a_rs, z_ss, z_rs, x_ss, x_rs, s_ss, s_rs, f_ss, f_rs,
+    d_ss, d_rs, y_ss, y_rs,
+):
+    f32, bf16 = jnp.float32, jnp.bfloat16
+    z, x, c = lax.axis_index("row"), lax.axis_index("head"), lax.axis_index("sub")
+    tokens, share = out_ref.shape
+    rows = tokens // STEPS
+    heads, wide = gain_b.shape
+    hidden_width = wg_b.shape[2]
+    width = 4 * share
+    own, sib = 2 * x + c, 2 * x + 1 - c
+    far, cross = 2 * (1 - x) + c, 2 * (1 - x) + 1 - c
+    sibling, opposite = {"sub": 1 - c}, {"head": 1 - x}
+    mesh_id = pl.DeviceIdType.MESH
+
+    def part(index):
+        return pl.ds(pl.multiple_of(index * share, 128), share)
+
+    def row_part(index):
+        return pl.ds(pl.multiple_of(index * tokens, 16), tokens)
+
+    def remote(src, dst, ss, rs, where):
+        return pltpu.make_async_remote_copy(
+            src_ref=src, dst_ref=dst, send_sem=ss, recv_sem=rs,
+            device_id=where, device_id_type=mesh_id,
+        )
+
+    smalls = [
+        (q_h, q_b), (k_h, k_b), (v_h, v_b), (g_h, g_b), (gain_h, gain_b),
+        (res_h.at[:, part(own)], res_b), (fgain_h.at[:, part(own)], fgain_b),
+        (router_h, router_b), (meta_h, facts_b.at[row_part(z), :]),
+    ]
+    small_copies = [
+        pltpu.make_async_copy(a, b, small_sem.at[i]) for i, (a, b) in enumerate(smalls)
+    ]
+    state_copy = pltpu.make_async_copy(state_h, state_b, state_sem.at[0])
+    out_order = (cross, sib, far, own)
+    in_order = (own, sib, far, cross)
+    wo_copies = [
+        pltpu.make_async_copy(wo_h.at[:, part(j)], wo_b.at[i], wo_sem.at[i])
+        for i, j in enumerate(out_order)
+    ]
+    wg_copies = [
+        pltpu.make_async_copy(wg_h.at[part(j), :], wg_b.at[i], wg_sem.at[i])
+        for i, j in enumerate(in_order)
+    ]
+    wu_copies = [
+        pltpu.make_async_copy(wu_h.at[part(j), :], wu_b.at[i], wu_sem.at[i])
+        for i, j in enumerate(in_order)
+    ]
+    wd_copies = [
+        pltpu.make_async_copy(wd_h.at[:, part(j)], wd_b.at[i], wd_sem.at[i])
+        for i, j in enumerate(out_order)
+    ]
+    for copy in small_copies:
+        copy.start()
+    state_copy.start()
+    for copy in wo_copies:
+        copy.start()
+    for i in range(4):
+        wg_copies[i].start()
+        wu_copies[i].start()
+    for copy in wd_copies:
+        copy.start()
+
+    barrier = pltpu.get_barrier_semaphore()
+    peers = [{"row": lax.rem(z + d, n)} for d in range(1, n)] + [sibling, opposite]
+    for peer in peers:
+        pl.semaphore_signal(barrier, inc=1, device_id=peer, device_id_type=mesh_id)
+
+    for copy in small_copies:
+        copy.wait()
+    q32[...] = q_b[...].astype(f32)
+    k32[...] = k_b[...].astype(f32)
+    v32[...] = v_b[...].astype(f32)
+    g32[...] = g_b[...].astype(f32)
+    state_copy.wait()
+    row_ids = lax.broadcasted_iota(jnp.int32, (tokens, 128), 0) % rows
+    squares = jnp.zeros((tokens, wide), f32)
+    pending = None
+    for h in range(heads):
+        picked = pl.ds(h, tokens, stride=heads)
+        q, k, v, g = q32[picked, :], k32[picked, :], v32[picked, :], g32[picked, :]
+        table = state_b[:, h, :, :].astype(bf16).reshape(rows * wide, state_b.shape[3])
+        read = lax.dot_general(
+            q.astype(bf16), table, (((1,), (1,)), ((), ())), preferred_element_type=f32
+        )
+        pairs = jnp.zeros((tokens, 2 * wide), f32)
+        for p in range(rows // 2):
+            pairs = jnp.where(row_ids // 2 == p, read[:, p * 128 : (p + 1) * 128], pairs)
+        kept = jnp.where(row_ids[:, :wide] % 2 == 0, pairs[:, :wide], pairs[:, wide:])
+        d = decay_s[0, h]
+        one = lambda s, t: jnp.sum(
+            q[s * rows : (s + 1) * rows] * k[t * rows : (t + 1) * rows], axis=1, keepdims=True
+        )
+        v0, v1 = v[:rows], v[rows:]
+        first = d * kept[:rows] + one(0, 0) * v0
+        second = d * (d * kept[rows:] + one(1, 0) * v0) + one(1, 1) * v1
+        attended = jnp.concatenate([first, second], axis=0)
+        squares = squares + attended * attended
+        gated = attended * gain_b[h : h + 1, :] * jax.nn.sigmoid(g)
+        if h % 2 == 0:
+            pending = gated
+        else:
+            both = jnp.concatenate([pending, gated], axis=1)
+            gated_b[:, (h // 2) * 128 : (h // 2 + 1) * 128] = both.astype(bf16)
+    square_part = jnp.sum(squares, axis=1, keepdims=True)
+    lanes = lax.broadcasted_iota(jnp.int32, (tokens, 128), 1)
+
+    pl.semaphore_wait(barrier, n + 1)
+    facts_copies = []
+    for d in range(1, n):
+        copy = remote(
+            facts_b.at[row_part(z), :], facts_b.at[row_part(z), :],
+            facts_ss.at[d - 1], facts_rs.at[d - 1], {"row": lax.rem(z + d, n)},
+        )
+        copy.start()
+        facts_copies.append(copy)
+
+    def project(i):
+        wo_copies[i].wait()
+        return jnp.dot(gated_b[...], wo_b[i], preferred_element_type=f32)
+
+    def a_pack(slot, value, column):
+        a_send[slot, :, :share] = value.astype(bf16)
+        a_send[slot, :, share:] = high_low(column, lanes).astype(bf16)
+
+    a_copies = [
+        remote(a_send.at[i], a_recv.at[i], a_ss.at[i], a_rs.at[i], where)
+        for i, where in enumerate((sibling, sibling, opposite))
+    ]
+    for i in range(2):
+        a_pack(i, project(i), square_part)
+        a_copies[i].start()
+    value = project(2)
+    a_copies[0].wait_recv()
+    a_pack(
+        2, value + a_recv[0, :, :share].astype(f32), square_part + column_of(a_recv[0, :, share:])
+    )
+    a_copies[2].start()
+    value = project(3)
+    a_copies[1].wait_recv()
+    value = value + a_recv[1, :, :share].astype(f32)
+    a_copies[2].wait_recv()
+    value = value + a_recv[2, :, :share].astype(f32)
+    total_square = (
+        square_part + column_of(a_recv[1, :, share:]) + column_of(a_recv[2, :, share:])
+    )
+    mixed = res_b[...].astype(f32) + value * lax.rsqrt(
+        total_square / (HEADS * HEAD_DIM) + EPSILON
+    )
+    mix_b[...] = mixed
+    mixed_square = jnp.sum(mixed * mixed, axis=1, keepdims=True)
+    x_all[own, row_part(z), :share] = (mixed * fgain_b[...]).astype(bf16)
+    x_all[own, row_part(z), share:] = high_low(mixed_square, lanes).astype(bf16)
+
+    def block(j, d):
+        return x_all.at[j, row_part(lax.rem(z - d + n, n)), :]
+
+    z_copies = [
+        remote(block(own, 0), block(own, 0), z_ss.at[d - 1], z_rs.at[d - 1],
+               {"row": lax.rem(z + d, n)})
+        for d in range(1, n)
+    ]
+    x_copies = [
+        remote(block(own, d), block(own, d), x_ss.at[d], x_rs.at[d], opposite) for d in range(n)
+    ]
+    s_copies = [
+        remote(block(own, d), block(own, d), s_ss.at[d], s_rs.at[d], sibling) for d in range(n)
+    ]
+    f_copies = [
+        remote(block(far, d), block(far, d), f_ss.at[d], f_rs.at[d], sibling) for d in range(n)
+    ]
+    for copy in z_copies:
+        copy.start()
+    x_copies[0].start()
+    s_copies[0].start()
+    for d in range(1, n):
+        z_copies[d - 1].wait_recv()
+        x_copies[d].start()
+        s_copies[d].start()
+
+    chunk = 512
+    scores = [jnp.zeros((n * tokens, 1), f32) for _ in range(experts)]
+    mean_sum = jnp.zeros((n * tokens, 1), f32)
+    for i, j in enumerate(in_order):
+        if i == 1:
+            for d in range(n):
+                x_copies[d].wait_recv()
+                f_copies[d].start()
+            for d in range(n):
+                s_copies[d].wait_recv()
+        if i == 3:
+            for d in range(n):
+                f_copies[d].wait_recv()
+        wg_copies[i].wait()
+        wu_copies[i].wait()
+        left = x_all[j, :, :share]
+        for m in range(hidden_width // chunk):
+            columns = pl.ds(m * chunk, chunk)
+            gate_term = jnp.dot(left, wg_b[i, :, columns], preferred_element_type=f32)
+            up_term = jnp.dot(left, wu_b[i, :, columns], preferred_element_type=f32)
+            if i == 0:
+                acc_g[:, columns] = gate_term
+                acc_u[:, columns] = up_term
+            else:
+                acc_g[:, columns] += gate_term
+                acc_u[:, columns] += up_term
+        wide_left = left.astype(f32)
+        mean_sum = mean_sum + column_of(x_all[j, :, share:])
+        for e in range(experts):
+            weights = router_b[e : e + 1, part(j)].astype(f32)
+            scores[e] = scores[e] + jnp.sum(wide_left * weights, axis=1, keepdims=True)
+
+    for copy in facts_copies:
+        copy.wait_recv()
+    facts = facts_b[...]
+    scale = lax.rsqrt(mean_sum / width + EPSILON)
+    pick_a, pick_b = facts[:, 0:1], facts[:, 1:2]
+    gap = jnp.zeros_like(scale)
+    for e in range(experts):
+        gap = gap + jnp.where(pick_a == e, scores[e], 0.0) - jnp.where(pick_b == e, scores[e], 0.0)
+    gap = gap * scale
+    mine = (z // (n // experts)).astype(f32)
+    share_of = jnp.where(pick_a == mine, jax.nn.sigmoid(gap), 0.0) + jnp.where(
+        pick_b == mine, jax.nn.sigmoid(-gap), 0.0
+    )
+    share_of = share_of * (1.0 - facts[:, 2:3])
+
+    def mover_of(entries, first_step_rows):
+        count = entries.shape[0]
+        field = lax.broadcasted_iota(jnp.int32, (n * tokens, 128), 1)
+        picker = jnp.where(field == 3, 1.0, 0.0).astype(bf16)
+        slots = lax.dot_general(
+            picker, entries.astype(bf16), (((1,), (1,)), ((), ())), preferred_element_type=f32
+        )
+        place = lax.broadcasted_iota(jnp.int32, (n * tokens, count), 0)
+        source = lax.broadcasted_iota(jnp.int32, (n * tokens, count), 1)
+        same = (place // rows) % STEPS == (source // rows) % STEPS
+        slot = (place // tokens * rows + place % rows).astype(f32)
+        return jnp.where(same & (slots == slot), 1.0, 0.0).astype(bf16)
+
+    mover = mover_of(facts, None)
+    for m in range(hidden_width // chunk):
+        columns = pl.ds(m * chunk, chunk)
+        gate_pre = acc_g[:, columns] * scale
+        upward = acc_u[:, columns] * scale
+        hidden = (gate_pre * jax.nn.sigmoid(gate_pre) * upward * share_of).astype(bf16)
+        hid_b[:, columns] = jnp.dot(mover, hidden, preferred_element_type=f32).astype(bf16)
+
+    def lower(i, y):
+        wd_copies[i].wait()
+        return jnp.dot(hid_b[...], wd_b[i], preferred_element_type=f32)
+
+    d_copies = [
+        remote(d_send.at[i], d_recv.at[i], d_ss.at[i], d_rs.at[i], where)
+        for i, where in enumerate((sibling, sibling, opposite))
+    ]
+    for i in range(2):
+        d_send[i] = lower(i, None).astype(bf16)
+        d_copies[i].start()
+    value = lower(2, None)
+    d_copies[0].wait_recv()
+    d_send[2] = (value + d_recv[0].astype(f32)).astype(bf16)
+    d_copies[2].start()
+    value = lower(3, None)
+    own_facts = facts_b[row_part(z), :]
+    own_mover = mover_of(own_facts, None)
+    kept_mix = mix_b[...] * (1.0 - own_facts[:, 2:3])
+    mix_high = kept_mix.astype(bf16)
+    mix_low = (kept_mix - mix_high.astype(f32)).astype(bf16)
+    value = value + jnp.dot(own_mover, mix_high, preferred_element_type=f32)
+    value = value + jnp.dot(own_mover, mix_low, preferred_element_type=f32)
+    d_copies[1].wait_recv()
+    value = value + d_recv[1].astype(f32)
+    d_copies[2].wait_recv()
+    value = value + d_recv[2].astype(f32)
+    y_b[...] = value
+    y_send[...] = value.astype(bf16)
+    y_copies = []
+    for d in range(1, n):
+        there = lax.rem(z + d, n)
+        copy = remote(
+            y_send.at[row_part(there), :], y_recv.at[d - 1], y_ss.at[d - 1], y_rs.at[d - 1],
+            {"row": there},
+        )
+        copy.start()
+        y_copies.append(copy)
+    total = y_b[row_part(z), :]
+    for d in range(1, n):
+        y_copies[d - 1].wait_recv()
+        total = total + y_recv[d - 1].astype(f32)
+    out_ref[...] = total.astype(bf16)
+    for copy in (
+        facts_copies + a_copies + z_copies + x_copies + s_copies + f_copies + d_copies + y_copies
+    ):
+        copy.wait_send()
+
+
+def fused_local(
+    prior_state,
+    queries,
+    new_keys,
+    new_values,
+    out_gates,
+    decay_rates,
+    norm_gain,
+    out_weight,
+    residual,
+    ffn_gain,
+    router_weight,
+    gate_weight,
+    up_weight,
+    down_weight,
+    expert_picks,
+    finished,
+    dest_slots,
+):
+    f32, bf16 = jnp.float32, jnp.bfloat16
+    n = lax.axis_size("row")
+    rows, heads, key_dim = queries.shape[1:]
+    wide = new_values.shape[3]
+    width = residual.shape[2]
+    share = width // 4
+    experts = router_weight.shape[1]
+    hidden = gate_weight.shape[1]
+    tokens = STEPS * rows
+    flat = tokens * heads
+    facts = jnp.concatenate(
+        [expert_picks, finished[:, :, None], dest_slots[:, :, None]], axis=2
+    ).reshape(tokens, 4)
+    facts = jnp.pad(facts.astype(f32), ((0, 0), (0, 124)))
+    any_space = pl.BlockSpec(memory_space=pl.ANY)
+    dma = pltpu.SemaphoreType.DMA
+    out = pl.pallas_call(
+        functools.partial(fused_kernel, n, experts),
+        out_shape=jax.ShapeDtypeStruct((tokens, share), bf16),
+        in_specs=[pl.BlockSpec(memory_space=pltpu.SMEM)] + [any_space] * 14,
+        out_specs=pl.BlockSpec(memory_space=pltpu.VMEM),
+        scratch_shapes=[
+            pltpu.VMEM((flat, key_dim), bf16),
+            pltpu.VMEM((flat, key_dim), bf16),
+            pltpu.VMEM((flat, wide), bf16),
+            pltpu.VMEM((flat, wide), bf16),
+            pltpu.VMEM((heads, wide), f32),
+            pltpu.VMEM((tokens, share), bf16),
+            pltpu.VMEM((1, share), f32),
+            pltpu.VMEM((experts, width), bf16),
+            pltpu.VMEM((rows, heads, wide, key_dim), f32),
+            pltpu.VMEM((4, heads * wide, share), bf16),
+            pltpu.VMEM((4, share, hidden), bf16),
+            pltpu.VMEM((4, share, hidden), bf16),
+            pltpu.VMEM((4, hidden, share), bf16),
+            pltpu.VMEM((flat, key_dim), f32),
+            pltpu.VMEM((flat, key_dim), f32),
+            pltpu.VMEM((flat, wide), f32),
+            pltpu.VMEM((flat, wide), f32),
+            pltpu.VMEM((tokens, heads * wide), bf16),
+            pltpu.VMEM((n * tokens, 128), f32),
+            pltpu.VMEM((tokens, share), f32),
+            pltpu.VMEM((3, tokens, share + 128), bf16),
+            pltpu.VMEM((3, tokens, share + 128), bf16),
+            pltpu.VMEM((4, n * tokens, share + 128), bf16),
+            pltpu.VMEM((n * tokens, hidden), f32),
+            pltpu.VMEM((n * tokens, hidden), f32),
+            pltpu.VMEM((n * tokens, hidden), bf16),
+            pltpu.VMEM((3, n * tokens, share), bf16),
+            pltpu.VMEM((3, n * tokens, share), bf16),
+            pltpu.VMEM((n * tokens, share), f32),
+            pltpu.VMEM((n * tokens, share), bf16),
+            pltpu.VMEM((n - 1, tokens, share), bf16),
+            dma((9,)), dma((1,)), dma((4,)), dma((4,)), dma((4,)), dma((4,)),
+            dma((n - 1,)), dma((n - 1,)), dma((3,)), dma((3,)), dma((n - 1,)), dma((n - 1,)),
+            dma((n,)), dma((n,)), dma((n,)), dma((n,)), dma((n,)), dma((n,)),
+            dma((3,)), dma((3,)), dma((n - 1,)), dma((n - 1,)),
+        ],
+        compiler_params=pltpu.CompilerParams(
+            collective_id=0, has_side_effects=True, vmem_limit_bytes=58 * 1024 * 1024
+        ),
+    )(
+        decay_rates.reshape(1, heads),
+        queries.reshape(flat, key_dim),
+        new_keys.reshape(flat, key_dim),
+        new_values.reshape(flat, wide),
+        out_gates.reshape(flat, wide),
+        norm_gain,
+        residual.reshape(tokens, width),
+        ffn_gain.reshape(1, width),
+        router_weight.T,
+        facts,
+        jnp.swapaxes(prior_state, 2, 3),
+        out_weight.reshape(heads * wide, width),
+        gate_weight,
+        up_weight,
+        down_weight,
+    )
+    return out.reshape(STEPS, rows, share)
+
+
 def solution(mesh):
     in_specs = (
         P(("group", "row"), "head", None, "sub"),
@@ -121,4 +545,6 @@
         P(None, ("group", "row")),
     )
     out_specs = P(None, ("group", "row"), ("head", "sub"))
-    return jax.shard_map(local, mesh=mesh, in_specs=in_specs, out_specs=out_specs, check_vma=False)
+    small = mesh.shape["head"] == 2 and mesh.shape["sub"] == 2 and mesh.shape["row"] in (4, 8)
+    part_program = fused_local if small else local
+    return jax.shard_map(part_program, mesh=mesh, in_specs=in_specs, out_specs=out_specs, check_vma=False)

time: 145 us -> 49.5 us (0.34)
  waiting for transfers between devices: 57 us -> 0 us
  Pallas kernels: 0 us -> 44.9 us
  blocking collectives: 34.8 us -> 0 us
  matrix products: 31.6 us -> 0 us
  between operations: 13.2 us -> 0.01 us
  other arithmetic: 7.22 us -> 0.01 us
  local copies, waits for them, and re-layouts: 0.75 us -> 4.32 us
    pallas_call x0 -> x1, Pallas kernels: none -> 44.9 us  [fused_local(): pl.pallas_call(functools.partial(fused_kernel, n, experts), out_shape=jax...]
    reduce_scatter x2 -> x0, waiting for transfers between devices: 43.4 us -> none  [the longest x1 23.6 us: local(): lax.psum_scatter(produced, ('head', 'sub'), scatter_dimension=1, tiled=True)]
    dot_general x7 -> x0, matrix products: 31.6 us -> none  [the longest x1 7.94 us: local(): produced = jnp.dot(hidden, down_weight, preferred_element_type=f32)]
    all_gather x2 -> x0, blocking collectives: 26.5 us -> none  [the longest x1 14.4 us: local(): everyone = lax.all_gather(normed, 'row', axis=0, tiled=True)]
    psum x1 -> x0, waiting for transfers between devices: 13.6 us -> none  [local(): lax.psum((partial, squares.reshape(STEPS * rows)), ('head', 'sub'))]
    psum x1 -> x0, blocking collectives: 8.31 us -> none  [local(): lax.psum((partial, squares.reshape(STEPS * rows)), ('head', 'sub'))]
    convert_element_type x5 -> x1, other arithmetic: 2.7 us -> 0.01 us  [fused_local(): facts = jnp.pad(facts.astype(f32), ((0, 0), (0, 124)))]
    reduce_sum x3 -> x0, other arithmetic: 2.27 us -> none  [the longest x1 1.14 us: local(): jnp.mean(mixed * mixed, axis=1, keepdims=True) + EPSILON]
  transfers between devices with their start and end apart: 3 -> 0, of which waited for: 3 -> 0; matrix products, arithmetic and copies ran while one was open for 0% -> 0% of each run, Pallas kernels for 0% -> 0%
where the time goes in v2:
time: 49.5 us; the launch traced here: 49.3 us
  Pallas kernels  44.9 us (91%)
  local copies, waits for them, and re-layouts  4.32 us (9%)
    pallas_call x1, Pallas kernels, fused_local(): pl.pallas_call(functools.partial(fused_kernel, n, experts), out_shape=jax...  44.9 us
    unnamed x2, local copies, waits for them, and re-layouts  2.03 us
    concatenate x3, local copies, waits for them, and re-layouts, fused_local(): jnp.concatenate([expert_picks, finished[:, :, None], dest_slots[:, :, Non...  1.6 us

profile of v2, /device:TPU:0, one launch (start us, length us, event | category | flops | bytes accessed | tf_op | source)
XLA Modules:
  0.0 49.3 jit_solution(2181299038402774325)
XLA Ops:
  0.0 0.8 %concatenate.11 = s32[16,1]{0,1:T(1,128)S(1)} reshape(s32[2,8]{1,0:T(2,128)} %param.32) | data formatting | bytes 128 | tf_op jit(solution)/shard_map/concatenate | solution.py:456
  0.8 0.8 %concatenate.12 = s32[16,1]{0,1:T(1,128)S(1)} reshape(s32[2,8]{1,0:T(2,128)} %param.33) | data formatting | bytes 128 | tf_op jit(solution)/shard_map/concatenate | solution.py:456
  1.5 0.7 %copy.24 = s32[2,8,2]{1,0,2:T(2,128)S(1)} copy(s32[2,8,2]{1,2,0:T(2,128)} %param.31) | data formatting | bytes 256 | tf_op args[14]
  2.2 0.1 concatenate.10
  2.3 0.1 copy.25
  2.4 0.6 %pad.4.meta_h = f32[16,128]{1,0:T(8,128)} pad(f32[16,4]{1,0:T(8,128)S(1)} %copy.25, f32[]{:T(128)} %constant.2.clone.1), padding=0_0x0_124 | pad | bytes 8452 | tf_op jit(solution)/shard_map/jit(_pad)/pad | solution.py:459
  3.0 44.9 %shard_map.163 = bf16[16,768]{1,0:T(8,128)(2,1)} custom-call(f32[1,16]{1,0:T(1,128)} %bitcast.23, bf16[256,128]{1,0:T(8,128)(2,1)} %bitcast.17, bf16[256,128]{1,0:T(8,128)(2,1)} %bitcast.18, bf16[256,64]{1,0:T(8,128)(2,1)} %bitcast.19, bf16[256,64]{1,0:T(8,128)(2,1)} %bitcast.20, f32[16,64]{1,0:T(8,128)} %gain_h.1, bf16[16,3072]{1,0:T(8,128)(2,1)} %bitcast.15, ...), custom_call_target="tpu_custom_call" | custom-call | tf_op jit(solution)/shard_map/pallas_call | solution.py:462
  47.9 1.3 %copy.27 = bf16[2,8,768]{2,1,0:T(8,128)(2,1)} copy(bf16[2,8,768]{2,1,0:T(8,128)(2,1)} %bitcast.16) | data formatting | bytes 49152
  (1 shorter events, 0.0 us)

commit v3 on v2

--- a/solution.py
+++ b/solution.py
@@ -184,11 +184,6 @@
     state_copy.start()
     for copy in wo_copies:
         copy.start()
-    for i in range(4):
-        wg_copies[i].start()
-        wu_copies[i].start()
-    for copy in wd_copies:
-        copy.start()
 
     barrier = pltpu.get_barrier_semaphore()
     peers = [{"row": lax.rem(z + d, n)} for d in range(1, n)] + [sibling, opposite]
@@ -202,6 +197,9 @@
     v32[...] = v_b[...].astype(f32)
     g32[...] = g_b[...].astype(f32)
     state_copy.wait()
+    for i in range(4):
+        wg_copies[i].start()
+        wu_copies[i].start()
     row_ids = lax.broadcasted_iota(jnp.int32, (tokens, 128), 0) % rows
     squares = jnp.zeros((tokens, wide), f32)
     pending = None
@@ -308,6 +306,8 @@
         s_copies[d].start()
 
     chunk = 512
+    for copy in wd_copies:
+        copy.start()
     scores = [jnp.zeros((n * tokens, 1), f32) for _ in range(experts)]
     mean_sum = jnp.zeros((n * tokens, 1), f32)
     for i, j in enumerate(in_order):
@@ -453,10 +453,12 @@
     hidden = gate_weight.shape[1]
     tokens = STEPS * rows
     flat = tokens * heads
-    facts = jnp.concatenate(
-        [expert_picks, finished[:, :, None], dest_slots[:, :, None]], axis=2
-    ).reshape(tokens, 4)
-    facts = jnp.pad(facts.astype(f32), ((0, 0), (0, 124)))
+    lane = lax.broadcasted_iota(jnp.int32, (STEPS, rows, 128), 2)
+    facts = jnp.zeros((STEPS, rows, 128), jnp.int32)
+    fields = (expert_picks[:, :, 0], expert_picks[:, :, 1], finished, dest_slots)
+    for index, field in enumerate(fields):
+        facts = jnp.where(lane == index, field[:, :, None], facts)
+    facts = facts.astype(f32).reshape(tokens, 128)
     any_space = pl.BlockSpec(memory_space=pl.ANY)
     dma = pltpu.SemaphoreType.DMA
     out = pl.pallas_call(

time: 49.5 us -> 41.6 us (0.84)
  Pallas kernels: 44.9 us -> 36.9 us
  other arithmetic: 0.01 us -> 0.69 us
  local copies, waits for them, and re-layouts: 4.32 us -> 3.8 us
    pallas_call x1, Pallas kernels: 44.9 us -> 36.9 us  [fused_local(): pl.pallas_call(functools.partial(fused_kernel, n, experts), out_shape=jax...]
    broadcast_in_dim x0 -> x4, local copies, waits for them, and re-layouts: none -> 1.68 us  [fused_local(): facts = jnp.where(lane == index, field[:, :, None], facts)]
    concatenate x3 -> x0, local copies, waits for them, and re-layouts: 1.6 us -> none  [fused_local(): jnp.concatenate([expert_picks, finished[:, :, None], dest_slots[:, :, Non...]
    slice x0 -> x1, local copies, waits for them, and re-layouts: none -> 0.78 us  [fused_local(): expert_picks[:, :, 1]]
    unnamed x2 -> x1, local copies, waits for them, and re-layouts: 2.03 us -> 1.35 us
    convert_element_type x1, other arithmetic: 0.01 us -> 0.68 us  [fused_local(): facts = facts.astype(f32).reshape(tokens, 128)]
    pad x1 -> x0, local copies, waits for them, and re-layouts: 0.6 us -> none  [fused_local(): facts = jnp.pad(facts.astype(f32), ((0, 0), (0, 124)))]
where the time goes in v3:
time: 41.6 us; the launch traced here: 41.4 us
  Pallas kernels  36.9 us (89%)
  local copies, waits for them, and re-layouts  3.8 us (9%)
  other arithmetic  0.69 us (2%)
    pallas_call x1, Pallas kernels, fused_local(): pl.pallas_call(functools.partial(fused_kernel, n, experts), out_shape=jax...  36.9 us
    broadcast_in_dim x4, local copies, waits for them, and re-layouts, fused_local(): facts = jnp.where(lane == index, field[:, :, None], facts)  1.68 us
    unnamed x1, local copies, waits for them, and re-layouts  1.35 us

profile of v3, /device:TPU:0, one launch (start us, length us, event | category | flops | bytes accessed | tf_op | source)
XLA Modules:
  0.0 41.4 jit_solution(3079134440233302471)
XLA Ops:
  0.0 0.8 %broadcast_in_dim.35 = s32[16]{0:T(128)S(1)} reshape(s32[2,8]{1,0:T(2,128)} %param.32) | data formatting | bytes 128 | tf_op jit(solution)/shard_map/jit(_where)/broadcast_in_dim | solution.py:460
  0.8 0.8 %broadcast_in_dim.33 = s32[16]{0:T(128)S(1)} reshape(s32[2,8]{1,0:T(2,128)} %param.33) | data formatting | bytes 128 | tf_op jit(solution)/shard_map/jit(_where)/broadcast_in_dim | solution.py:460
  1.5 0.8 %slice_reduce_fusion.1 = (s32[2,8]{1,0:T(2,128)S(1)}, s32[2,8]{1,0:T(2,128)S(1)}) fusion(s32[2,8,2]{1,2,0:T(2,128)} %param.31), kind=kLoop, calls=%fused_computation.2 | loop fusion | bytes 256 | tf_op jit(solution)/shard_map/slice | solution.py:458
  2.3 0.1 broadcast_in_dim.37
  2.4 0.1 broadcast_in_dim.39
  2.5 0.7 %select_convert_fusion.meta_h = f32[16,128]{1,0:T(8,128)} fusion(s32[16]{0:T(128)S(1)} %broadcast_in_dim.39, s32[16]{0:T(128)S(1)} %broadcast_in_dim.37, s32[16]{0:T(128)S(1)} %broadcast_in_dim.35, s32[16]{0:T(128)S(1)} %broadcast_in_dim.33, pred[128]{0:T(512)(128)(4,1)S(1)} %get-tuple-element.7, pred[128]{0:T(512)(128)(4,1)S(1)} %get-tuple-element.8, ...), kind=kLoop, calls=%fused_computation | loop fusion | flops 10240 | bytes 8960 | tf_op jit(solution)/shard_map/convert_element_type | solution.py:461
  3.2 36.9 %shard_map.163 = bf16[16,768]{1,0:T(8,128)(2,1)} custom-call(f32[1,16]{1,0:T(1,128)} %bitcast.21, bf16[256,128]{1,0:T(8,128)(2,1)} %bitcast.15, bf16[256,128]{1,0:T(8,128)(2,1)} %bitcast.16, bf16[256,64]{1,0:T(8,128)(2,1)} %bitcast.17, bf16[256,64]{1,0:T(8,128)(2,1)} %bitcast.18, f32[16,64]{1,0:T(8,128)} %gain_h.1, bf16[16,3072]{1,0:T(8,128)(2,1)} %bitcast.13, ...), custom_call_target="tpu_custom_call" | custom-call | tf_op jit(solution)/shard_map/pallas_call | solution.py:464
  40.0 1.3 %copy.19 = bf16[2,8,768]{2,1,0:T(8,128)(2,1)} copy(bf16[2,8,768]{2,1,0:T(8,128)(2,1)} %bitcast.14) | data formatting | bytes 49152
  (2 shorter events, 0.0 us)
